TPU v7x, 32 devices: a whole 2x2x4 slice. The times are simulated.
32 devices in a mesh: groups: 2 (over y), pairs: 4 (over z), rhs: 4 (over x, core).
Axes of the slice: x: 2, y: 2, z: 4, core: 2. Of those that a mesh axis runs over, the one named last changes fastest.
Arguments:
- features: float32 [40, 12288], P(None, ('groups', 'pairs')), parts along dimension 1
- inv_scale: float32 [40], replicated, may hold values from 0.006 to 0.018
- cluster_order: int32 [12288], P(('groups', 'pairs')), parts along dimension 0, may hold values from 0 to 6143, as said below
- counts: int32 [8], P(('groups', 'pairs')), parts along dimension 0, may hold values from 384 to 1536, as said below
- tile_cols: int32 [24, 3], P('groups'), parts along dimension 0, may hold values from -1 to 11, as said below
- targets: float32 [32, 12288], P('rhs', ('groups', 'pairs')), parts along dimension 1, may hold values from -4 to 4
Outputs:
- solution: float32 [32, 12288], P('rhs', ('groups', 'pairs')), parts along dimension 1
- residual: float32 [32, 12288], P('rhs', ('groups', 'pairs')), parts along dimension 1
There are 2 independent parts, one for each index of `groups`. A program takes and returns all parts, laid end to end along the dimension named above; an argument that names none is the same for every part. Nothing has to cross between parts.
Inputs may be any that keep to these rules, and one draw needn't show every extreme that they name: `cluster_order`: each block of 1536 positions of the cluster ordering holds a permutation of the same block of input columns. `counts`: some block is full in every draw. `tile_cols`: row tile i lists i first, then 3 - 1 distinct tiles from i + 1 to i + 3; a tile past the last one is given as -1.
All inputs are finite; a program needn't handle non-finite values.
Results may differ from a plain program's by a relative error of at most 0.0003.
Values sent between devices are 32-bit elements; how exact they have to be, the bound alone decides.
A program may use at most 64 MiB of HBM per device.

v0:
```python
import functools
import math

import jax
import jax.numpy as jnp
from jax import lax
from jax.experimental import pallas as pl
from jax.experimental.pallas import tpu as pltpu
from jax.sharding import PartitionSpec as P

TILE = 512
BAND = 3
NT = 3
CHUNK = 64
FEAT = 40
DEPTH = 256

root_three = math.sqrt(3.0)
log2_e = math.log2(math.e)
f32 = jnp.float32
bf16 = jnp.bfloat16

OFF = ((0, 1, 0), (0, 2, 1), (1, 2, 0), (1, 3, 1), (2, 3, 0), (2, 4, 1))


def three_parts(x):
    hi = x.astype(bf16).astype(f32)
    rest = x - hi
    mid = rest.astype(bf16).astype(f32)
    low = (rest - mid).astype(bf16).astype(f32)
    return hi, mid, low


def operand(x, is_row):
    hi, mid, low = three_parts(x)
    sq = jnp.sum(x * x, axis=0, keepdims=True)
    sq_hi, sq_mid, sq_low = three_parts(sq)
    width = x.shape[1]
    row = lax.broadcasted_iota(jnp.int32, (8, width), 0)
    first = 0 if is_row else 3
    tail = jnp.where(row < 6, 1.0, 0.0)
    tail = jnp.where(row == first, sq_hi, tail)
    tail = jnp.where(row == first + 1, sq_mid, tail)
    tail = jnp.where(row == first + 2, sq_low, tail)
    zero = jnp.zeros((8, width), f32)
    if is_row:
        parts = [-2.0 * y for y in (hi, hi, mid, hi, low, mid)]
    else:
        parts = [hi, mid, hi, low, hi, mid]
    return jnp.concatenate(parts + [tail, zero], axis=0)


def two_parts(v):
    hi = v.astype(bf16).astype(f32)
    return jnp.concatenate([hi, v - hi], axis=0).astype(bf16)


def fold(t):
    half = t.shape[0] // 2
    return t[:half] + t[half:]


def body(
    n, strength, feat_ref, counts_ref, cols_ref, targ_ref, sol_ref, res_ref,
    up_feat, r_buf, up_r, w_buf, up_w, out1, in1, out2, in2, part1, got1, part2, got2,
    a_ref, b_ref, ds_ref, khi, klo, vec, send_sem, recv_sem, psend1, precv1, psend2, precv2,
):
    me = lax.axis_index("pairs")
    mesh_ids = pl.DeviceIdType.MESH
    p_slots = NT * TILE
    has_up = me < n - 1
    has_down = me > 0

    barrier = pltpu.get_barrier_semaphore()
    for k in range(1, n):
        pl.semaphore_signal(barrier, inc=1, device_id={"pairs": lax.rem(me + k, n)}, device_id_type=mesh_ids)

    lane = lax.broadcasted_iota(jnp.int32, (8, p_slots), 1)
    live = jnp.where(lane < counts_ref[0], 1.0, 0.0)
    r0 = targ_ref[...] * live
    r_buf[...] = r0

    @pl.when(jnp.logical_not(has_up))
    def _():
        up_feat[...] = jnp.zeros_like(up_feat)
        up_r[...] = jnp.zeros_like(up_r)
        up_w[...] = jnp.zeros_like(up_w)

    @pl.when(jnp.logical_not(has_down))
    def _():
        in1[...] = jnp.zeros_like(in1)
        in2[...] = jnp.zeros_like(in2)

    pl.semaphore_wait(barrier, n - 1)

    def shift(src, dst, slot, by):
        return pltpu.make_async_remote_copy(
            src_ref=src, dst_ref=dst, send_sem=send_sem.at[slot], recv_sem=recv_sem.at[slot],
            device_id={"pairs": lax.rem(me + by + n, n)}, device_id_type=mesh_ids,
        )

    c_feat = shift(feat_ref, up_feat, 0, -1)
    c_r = shift(r_buf, up_r, 1, -1)
    c_w = shift(w_buf, up_w, 2, -1)
    c_1 = shift(out1, in1, 3, 1)
    c_2 = shift(out2, in2, 4, 1)

    def when_start(cond, *copies):
        @pl.when(cond)
        def _():
            for c in copies:
                c.start()

    def when_recv(cond, *copies):
        @pl.when(cond)
        def _():
            for c in copies:
                c.wait_recv()

    when_start(has_down, c_r, c_feat)

    base = me * NT
    start, keep0, keep1 = [], [], []
    for row, cand, slot in OFF:
        a = cols_ref[base + row, 1]
        b = cols_ref[base + row, 2]
        a_in = jnp.where(a < 0, row + 3, a - base)
        b_in = jnp.where(b < 0, row + 3, b - base)
        if slot == 0:
            valid = jnp.maximum(a, b) >= 0
            c = jnp.minimum(jnp.minimum(a_in, b_in), cand + 1)
        else:
            valid = jnp.minimum(a, b) >= 0
            c = jnp.maximum(a_in, b_in)
        start.append(c)
        keep0.append(jnp.where(valid & (c == cand), 1.0, 0.0).astype(f32))
        keep1.append(jnp.where(valid & (c == cand + 1), 1.0, 0.0).astype(f32))

    def pick(ref, k, own):
        cand = OFF[k][1]
        lo = ref[:, cand * TILE : (cand + 1) * TILE]
        hi = ref[:, (cand + 1) * TILE : (cand + 2) * TILE]
        return jnp.where(start[k] == cand, lo, hi)

    for i in range(NT):
        span = slice(i * TILE, (i + 1) * TILE)
        x = feat_ref[:, span]
        a_ref[span, :] = operand(x, True).T.astype(bf16)
        b_ref[:, span] = operand(x, False).astype(bf16)

    def form(t, row, cols):
        ds_ref[...] = jnp.dot(a_ref[row * TILE : (row + 1) * TILE, :], cols, preferred_element_type=f32)

        def step(s, carry):
            at = pl.ds(pl.multiple_of(s * CHUNK, CHUNK), CHUNK)
            d2 = jnp.maximum(ds_ref[at, :], 0.0) + 1e-6
            d = d2 * lax.rsqrt(d2)
            env = jnp.maximum(1.0 - d, 0.0)
            k = (1.0 + root_three * d) * jnp.exp2((-root_three * log2_e) * d) * (env * env)
            hi = k.astype(bf16)
            khi[t, at, :] = hi
            klo[t, at, :] = (k - hi.astype(f32)).astype(bf16)
            return carry

        lax.fori_loop(0, TILE // CHUNK, step, 0)

    nt_dims = (((1,), (1,)), ((), ()))

    def to_rows(t, v):
        return fold(
            lax.dot_general(v, khi[t], nt_dims, preferred_element_type=f32)
            + lax.dot_general(v, klo[t], nt_dims, preferred_element_type=f32)
        )

    def to_cols(t, v):
        return fold(
            jnp.dot(v, khi[t], preferred_element_type=f32)
            + jnp.dot(v, klo[t], preferred_element_type=f32)
        )

    for i in range(NT):
        form(i, i, b_ref[:, i * TILE : (i + 1) * TILE])
    form(NT, 0, pick(b_ref, 0, True))
    when_recv(has_up, c_feat)
    for i in range(NT):
        span = slice(i * TILE, (i + 1) * TILE)
        b_ref[:, p_slots + i * TILE : p_slots + (i + 1) * TILE] = operand(up_feat[:, span], False).astype(bf16)
    for k in range(1, 6):
        form(NT + k, OFF[k][0], pick(b_ref, k, False))

    def own(i):
        return vec[:, i * TILE : (i + 1) * TILE]

    def operate(v, out_ref, c_out, up_ref, c_up, in_ref):
        vec[:, :p_slots] = two_parts(v)
        acc = [jnp.zeros((8, TILE), f32) for _ in range(2 * NT)]
        for k in range(1, 6):
            row, cand, _ = OFF[k]
            t = to_cols(NT + k, own(row))
            acc[cand] = acc[cand] + keep0[k] * t
            acc[cand + 1] = acc[cand + 1] + keep1[k] * t
        out_ref[...] = jnp.concatenate(acc[NT:], axis=1)
        when_start(has_up, c_out)
        for i in range(NT):
            acc[i] = acc[i] + to_rows(i, own(i))
        t = to_cols(NT, own(0))
        acc[1] = acc[1] + keep0[0] * t
        acc[2] = acc[2] + keep1[0] * t
        acc[0] = acc[0] + (keep0[0] + keep1[0]) * to_rows(NT, pick(vec, 0, True))
        when_recv(has_up, c_up)
        vec[:, p_slots:] = two_parts(up_ref[...])
        for k in range(1, 6):
            row = OFF[k][0]
            acc[row] = acc[row] + (keep0[k] + keep1[k]) * to_rows(NT + k, pick(vec, k, False))
        when_recv(has_down, c_out)
        total = jnp.concatenate(acc[:NT], axis=1) + in_ref[...]
        return v + strength * live * total

    def start_sums(first, second, part, got, ssem, rsem):
        part[0:8, :] = jnp.broadcast_to(jnp.sum(first, axis=1, keepdims=True), (8, 128))
        part[8:16, :] = jnp.broadcast_to(jnp.sum(second, axis=1, keepdims=True), (8, 128))
        copies = []
        for k in range(1, n):
            c = pltpu.make_async_remote_copy(
                src_ref=part, dst_ref=got.at[k - 1], send_sem=ssem.at[k - 1], recv_sem=rsem.at[k - 1],
                device_id={"pairs": lax.rem(me + k, n)}, device_id_type=mesh_ids,
            )
            c.start()
            copies.append(c)
        return copies

    def end_sums(copies, part, got):
        total = part[...]
        for k, c in enumerate(copies):
            c.wait_recv()
            total = total + got[k]
        return total[0:8, 0:1], total[8:16, 0:1]

    w = operate(r0, out1, c_1, up_r, c_r, in1)
    w_buf[...] = w
    when_start(has_down, c_w)
    sums1 = start_sums(r0 * r0, r0 * w, part1, got1, psend1, precv1)
    u = operate(w, out2, c_2, up_w, c_w, in2)
    norm0, curve0 = end_sums(sums1, part1, got1)
    step0 = norm0 / curve0
    r1 = r0 - step0 * w
    applied = w - step0 * u
    sums2 = start_sums(r1 * r1, r1 * applied, part2, got2, psend2, precv2)
    norm1, curve1 = end_sums(sums2, part2, got2)
    rescale = norm1 / norm0
    step1 = norm1 / (curve1 - rescale * norm1 / step0)
    sol_ref[...] = step0 * r0 + step1 * (r1 + rescale * r0)
    res_ref[...] = r1 - step1 * (applied + rescale * w)

    @pl.when(has_down)
    def _():
        for c in (c_feat, c_r, c_w):
            c.wait_send()

    @pl.when(has_up)
    def _():
        for c in (c_1, c_2):
            c.wait_send()

    for c in sums1 + sums2:
        c.wait_send()


def on_device(n, features, inv_scale, cluster_order, counts, tile_cols, targets):
    p_slots = features.shape[1]
    rhs_rows = targets.shape[0]
    shard_index = lax.axis_index("pairs")
    local_index = cluster_order - shard_index * p_slots
    ordered = jnp.take(features, local_index, axis=1) * inv_scale[:, None]
    strength = 0.95 / (2 * BAND * TILE)
    padded = targets
    if rhs_rows < 8:
        padded = jnp.concatenate([targets, jnp.ones((8 - rhs_rows, p_slots), f32)], axis=0)
    vmem = pl.BlockSpec(memory_space=pltpu.VMEM)
    smem = pl.BlockSpec(memory_space=pltpu.SMEM)
    field = pltpu.VMEM((8, p_slots), f32)
    dma = pltpu.SemaphoreType.DMA
    tiles = 9
    out = jax.ShapeDtypeStruct((8, p_slots), f32)
    sol, res = pl.pallas_call(
        functools.partial(body, n, strength),
        out_shape=(out, out),
        in_specs=[vmem, smem, smem, vmem],
        out_specs=(vmem, vmem),
        scratch_shapes=[
            pltpu.VMEM((FEAT, p_slots), f32),
            field, field, field, field, field, field, field, field,
            pltpu.VMEM((16, 128), f32),
            pltpu.VMEM((n - 1, 16, 128), f32),
            pltpu.VMEM((16, 128), f32),
            pltpu.VMEM((n - 1, 16, 128), f32),
            pltpu.VMEM((p_slots, DEPTH), bf16),
            pltpu.VMEM((DEPTH, 2 * p_slots), bf16),
            pltpu.VMEM((TILE, TILE), f32),
            pltpu.VMEM((tiles, TILE, TILE), bf16),
            pltpu.VMEM((tiles, TILE, TILE), bf16),
            pltpu.VMEM((16, 2 * p_slots), bf16),
            dma((5,)), dma((5,)),
            dma((n - 1,)), dma((n - 1,)), dma((n - 1,)), dma((n - 1,)),
        ],
        compiler_params=pltpu.CompilerParams(
            collective_id=0, has_side_effects=True, vmem_limit_bytes=48 * 2**20
        ),
    )(ordered, counts, tile_cols, padded)
    return sol[:rhs_rows], res[:rhs_rows]


def solution(mesh):
    return jax.shard_map(
        functools.partial(on_device, mesh.shape["pairs"]),
        mesh=mesh,
        in_specs=(
            P(None, ("groups", "pairs")),
            P(),
            P(("groups", "pairs")),
            P(("groups", "pairs")),
            P("groups", None),
            P("rhs", ("groups", "pairs")),
        ),
        out_specs=(P("rhs", ("groups", "pairs")), P("rhs", ("groups", "pairs"))),
        check_vma=False,
    )
```

profile of v0, /device:TPU:0, one launch (start us, length us, event | category | flops | bytes accessed | tf_op | source)
XLA Modules:
  0.0 38.2 jit_solution(3115765566238622786)
XLA Ops:
  0.6 0.0 copy-start.1
  0.6 0.7 %copy-done.1 = s32[1536]{0:T(1024)S(1)} copy-done((s32[1536]{0:T(1024)S(1)}, s32[1536]{0:T(1024)}, u32[]{:S(2)}) %copy-start.1) | copy-done | bytes 6168
  1.3 1.2 %copy.8 = f32[40,1536]{0,1:T(8,128)S(1)} copy(f32[40,1536]{1,0:T(8,128)} %param.6) | data formatting | bytes 491520 | tf_op args[0]
  2.6 2.6 %gather_fusion = f32[1536,40]{1,0:T(8,128)S(1)} fusion(f32[40,1536]{0,1:T(8,128)S(1)} %copy.8, s32[2048]{0:T(1024)S(1)} %pad_clamp_fusion), kind=kCustom, calls=%fused_computation | custom fusion | bytes 497664 | tf_op jit(solution)/shard_map/jit(_take)/gather | solution.py:274
  5.2 0.2 copy.9
  5.4 0.0 copy-start.3
  5.4 0.7 %copy-done.3 = f32[40]{0:T(128)S(1)} copy-done((f32[40]{0:T(128)S(1)}, f32[40]{0:T(128)}, u32[]{:S(2)}) %copy-start.3) | copy-done | bytes 184
  6.1 0.0 copy-start.2
  6.1 0.0 copy-start
  6.1 0.1 multiply_bitcast_fusion.feat_ref
  6.2 0.6 %copy-done.2 = s32[12,3]{0,1:T(4,128)S(1)} copy-done((s32[12,3]{0,1:T(4,128)S(1)}, s32[12,3]{0,1:T(4,128)}, u32[]{:S(2)}) %copy-start.2) | copy-done | bytes 168
  6.7 0.1 copy.10.cols_ref
  7.5 0.0 copy-done
  7.5 29.4 %shard_map.77 = (f32[8,1536]{1,0:T(8,128)S(1)}, f32[8,1536]{1,0:T(8,128)S(1)}) custom-call(f32[40,1536]{1,0:T(8,128)S(1)} %multiply_bitcast_fusion.feat_ref, s32[1]{0:T(128)S(6)} %copy.13.counts_ref, s32[12,3]{1,0:T(8,128)S(1)} %copy.10.cols_ref, f32[8,1536]{1,0:T(8,128)S(1)} %copy-done), custom_call_target="tpu_custom_call" | custom-call | tf_op jit(solution)/shard_map/pallas_call | solution.py:285
  36.9 0.6 %copy.14 = f32[8,1536]{1,0:T(8,128)} copy(f32[8,1536]{1,0:T(8,128)S(1)} %get-tuple-element.6) | data formatting | bytes 98304
  37.5 0.6 %copy.15 = f32[8,1536]{1,0:T(8,128)} copy(f32[8,1536]{1,0:T(8,128)S(1)} %get-tuple-element.7) | data formatting | bytes 98304
  (2 shorter events, 0.0 us)
Async XLA Ops:
  0.6 0.7 %copy-start.1 = (s32[1536]{0:T(1024)S(1)}, s32[1536]{0:T(1024)}, u32[]{:S(2)}) copy-start(s32[1536]{0:T(1024)} %param.8) | copy-start | bytes 18436
  5.4 0.7 %copy-start.3 = (f32[40]{0:T(128)S(1)}, f32[40]{0:T(128)}, u32[]{:S(2)}) copy-start(f32[40]{0:T(128)} %param.7) | copy-start | bytes 484
  6.1 0.7 %copy-start.2 = (s32[12,3]{0,1:T(4,128)S(1)}, s32[12,3]{0,1:T(4,128)}, u32[]{:S(2)}) copy-start(s32[12,3]{0,1:T(4,128)} %param.10) | copy-start | bytes 436
  6.1 1.4 %copy-start = (f32[8,1536]{1,0:T(8,128)S(1)}, f32[8,1536]{1,0:T(8,128)}, u32[]{:S(2)}) copy-start(f32[8,1536]{1,0:T(8,128)} %targ_ref.1) | copy-start | bytes 147460
where the time goes:
time: 38.4 us; the launch traced here: 38.2 us
  Pallas kernels  29.4 us (77%)
  local copies, waits for them, and re-layouts  7.31 us (19%)
  between operations  1.34 us (3%)
    pallas_call x1, Pallas kernels, on_device(): pl.pallas_call(functools.partial(body, n, strength), out_shape=(out, out)...  29.4 us
    unnamed x12, local copies, waits for them, and re-layouts  4.48 us
    gather x2, local copies, waits for them, and re-layouts, on_device(): ordered = jnp.take(features, local_index, axis=1) * inv_scale[:, None]  2.83 us

commit v1 on v0

--- a/solution.py
+++ b/solution.py
@@ -12,6 +12,7 @@
 BAND = 3
 NT = 3
 CHUNK = 64
+LANES = 128
 FEAT = 40
 DEPTH = 256
 
@@ -61,8 +62,8 @@
 
 
 def body(
-    n, strength, feat_ref, counts_ref, cols_ref, targ_ref, sol_ref, res_ref,
-    up_feat, r_buf, up_r, w_buf, up_w, out1, in1, out2, in2, part1, got1, part2, got2,
+    n, strength, raw_ref, scale_ref, order_ref, counts_ref, cols_ref, targ_ref, sol_ref, res_ref,
+    feat, up_feat, r_buf, up_r, w_buf, up_w, out1, in1, out2, in2, part1, got1, part2, got2,
     a_ref, b_ref, ds_ref, khi, klo, vec, send_sem, recv_sem, psend1, precv1, psend2, precv2,
 ):
     me = lax.axis_index("pairs")
@@ -91,6 +92,23 @@
         in1[...] = jnp.zeros_like(in1)
         in2[...] = jnp.zeros_like(in2)
 
+    diag = lax.broadcasted_iota(jnp.int32, (FEAT, FEAT), 0) == lax.broadcasted_iota(jnp.int32, (FEAT, FEAT), 1)
+    scale = jnp.sum(jnp.where(diag, jnp.broadcast_to(scale_ref[...], (FEAT, FEAT)), 0.0), axis=1, keepdims=True)
+
+    def gather_tile(i):
+        for c in range(TILE // LANES):
+            first = i * TILE + c * LANES
+            index = order_ref[:, first : first + LANES] - me * p_slots
+            index = jnp.broadcast_to(index, (FEAT, LANES))
+            group = lax.shift_right_logical(index, 7)
+            within = jnp.bitwise_and(index, LANES - 1)
+            got = jnp.zeros((FEAT, LANES), f32)
+            for s in range(p_slots // LANES):
+                part = jnp.take_along_axis(raw_ref[:, s * LANES : (s + 1) * LANES], within, axis=1)
+                got = jnp.where(group == s, part, got)
+            feat[i, :, c * LANES : (c + 1) * LANES] = got * scale
+
+    gather_tile(0)
     pl.semaphore_wait(barrier, n - 1)
 
     def shift(src, dst, slot, by):
@@ -99,11 +117,11 @@
             device_id={"pairs": lax.rem(me + by + n, n)}, device_id_type=mesh_ids,
         )
 
-    c_feat = shift(feat_ref, up_feat, 0, -1)
-    c_r = shift(r_buf, up_r, 1, -1)
-    c_w = shift(w_buf, up_w, 2, -1)
-    c_1 = shift(out1, in1, 3, 1)
-    c_2 = shift(out2, in2, 4, 1)
+    c_feat = [shift(feat.at[i], up_feat.at[i], 4 + i, -1) for i in range(NT)]
+    c_r = shift(r_buf, up_r, 0, -1)
+    c_w = shift(w_buf, up_w, 1, -1)
+    c_1 = shift(out1, in1, 2, 1)
+    c_2 = shift(out2, in2, 3, 1)
 
     def when_start(cond, *copies):
         @pl.when(cond)
@@ -117,7 +135,11 @@
             for c in copies:
                 c.wait_recv()
 
-    when_start(has_down, c_r, c_feat)
+    when_start(has_down, c_feat[0])
+    gather_tile(1)
+    when_start(has_down, c_feat[1])
+    gather_tile(2)
+    when_start(has_down, c_feat[2], c_r)
 
     base = me * NT
     start, keep0, keep1 = [], [], []
@@ -144,25 +166,21 @@
 
     for i in range(NT):
         span = slice(i * TILE, (i + 1) * TILE)
-        x = feat_ref[:, span]
+        x = feat[i]
         a_ref[span, :] = operand(x, True).T.astype(bf16)
         b_ref[:, span] = operand(x, False).astype(bf16)
 
     def form(t, row, cols):
-        ds_ref[...] = jnp.dot(a_ref[row * TILE : (row + 1) * TILE, :], cols, preferred_element_type=f32)
-
-        def step(s, carry):
-            at = pl.ds(pl.multiple_of(s * CHUNK, CHUNK), CHUNK)
-            d2 = jnp.maximum(ds_ref[at, :], 0.0) + 1e-6
+        ds_ref[t % 2] = jnp.dot(a_ref[row * TILE : (row + 1) * TILE, :], cols, preferred_element_type=f32)
+        for s in range(TILE // CHUNK):
+            at = slice(s * CHUNK, (s + 1) * CHUNK)
+            d2 = jnp.maximum(ds_ref[t % 2, at, :], 0.0) + 1e-6
             d = d2 * lax.rsqrt(d2)
             env = jnp.maximum(1.0 - d, 0.0)
             k = (1.0 + root_three * d) * jnp.exp2((-root_three * log2_e) * d) * (env * env)
             hi = k.astype(bf16)
             khi[t, at, :] = hi
             klo[t, at, :] = (k - hi.astype(f32)).astype(bf16)
-            return carry
-
-        lax.fori_loop(0, TILE // CHUNK, step, 0)
 
     nt_dims = (((1,), (1,)), ((), ()))
 
@@ -181,12 +199,11 @@
     for i in range(NT):
         form(i, i, b_ref[:, i * TILE : (i + 1) * TILE])
     form(NT, 0, pick(b_ref, 0, True))
-    when_recv(has_up, c_feat)
-    for i in range(NT):
-        span = slice(i * TILE, (i + 1) * TILE)
-        b_ref[:, p_slots + i * TILE : p_slots + (i + 1) * TILE] = operand(up_feat[:, span], False).astype(bf16)
-    for k in range(1, 6):
-        form(NT + k, OFF[k][0], pick(b_ref, k, False))
+    for i, pairs in ((0, (1, 2)), (1, (3, 4)), (2, (5,))):
+        when_recv(has_up, c_feat[i])
+        b_ref[:, p_slots + i * TILE : p_slots + (i + 1) * TILE] = operand(up_feat[i], False).astype(bf16)
+        for k in pairs:
+            form(NT + k, OFF[k][0], pick(b_ref, k, False))
 
     def own(i):
         return vec[:, i * TILE : (i + 1) * TILE]
@@ -254,7 +271,7 @@
 
     @pl.when(has_down)
     def _():
-        for c in (c_feat, c_r, c_w):
+        for c in (*c_feat, c_r, c_w):
             c.wait_send()
 
     @pl.when(has_up)
@@ -269,9 +286,6 @@
 def on_device(n, features, inv_scale, cluster_order, counts, tile_cols, targets):
     p_slots = features.shape[1]
     rhs_rows = targets.shape[0]
-    shard_index = lax.axis_index("pairs")
-    local_index = cluster_order - shard_index * p_slots
-    ordered = jnp.take(features, local_index, axis=1) * inv_scale[:, None]
     strength = 0.95 / (2 * BAND * TILE)
     padded = targets
     if rhs_rows < 8:
@@ -285,10 +299,11 @@
     sol, res = pl.pallas_call(
         functools.partial(body, n, strength),
         out_shape=(out, out),
-        in_specs=[vmem, smem, smem, vmem],
+        in_specs=[vmem, vmem, vmem, smem, smem, vmem],
         out_specs=(vmem, vmem),
         scratch_shapes=[
-            pltpu.VMEM((FEAT, p_slots), f32),
+            pltpu.VMEM((NT, FEAT, TILE), f32),
+            pltpu.VMEM((NT, FEAT, TILE), f32),
             field, field, field, field, field, field, field, field,
             pltpu.VMEM((16, 128), f32),
             pltpu.VMEM((n - 1, 16, 128), f32),
@@ -296,17 +311,17 @@
             pltpu.VMEM((n - 1, 16, 128), f32),
             pltpu.VMEM((p_slots, DEPTH), bf16),
             pltpu.VMEM((DEPTH, 2 * p_slots), bf16),
-            pltpu.VMEM((TILE, TILE), f32),
+            pltpu.VMEM((2, TILE, TILE), f32),
             pltpu.VMEM((tiles, TILE, TILE), bf16),
             pltpu.VMEM((tiles, TILE, TILE), bf16),
             pltpu.VMEM((16, 2 * p_slots), bf16),
-            dma((5,)), dma((5,)),
+            dma((7,)), dma((7,)),
             dma((n - 1,)), dma((n - 1,)), dma((n - 1,)), dma((n - 1,)),
         ],
         compiler_params=pltpu.CompilerParams(
             collective_id=0, has_side_effects=True, vmem_limit_bytes=48 * 2**20
         ),
-    )(ordered, counts, tile_cols, padded)
+    )(features, inv_scale[None, :], cluster_order[None, :], counts, tile_cols, padded)
     return sol[:rhs_rows], res[:rhs_rows]
 
 

time: 38.4 us -> 30.9 us (0.80)
  Pallas kernels: 29.4 us -> 25 us
  local copies, waits for them, and re-layouts: 7.31 us -> 4.35 us
    pallas_call x1, Pallas kernels: 29.4 us -> 25 us  [on_device(): pl.pallas_call(functools.partial(body, n, strength), out_shape=(out, out)...]
    gather x2 -> x0, local copies, waits for them, and re-layouts: 2.83 us -> none  [on_device(): ordered = jnp.take(features, local_index, axis=1) * inv_scale[:, None]]
    unnamed x12 -> x11, local copies, waits for them, and re-layouts: 4.48 us -> 3.64 us
    broadcast_in_dim x0 -> x1, local copies, waits for them, and re-layouts: none -> 0.71 us  [on_device(): cluster_order[None, :]]
where the time goes in v1:
time: 30.9 us; the launch traced here: 30.7 us
  Pallas kernels  25 us (81%)
  local copies, waits for them, and re-layouts  4.35 us (14%)
  between operations  1.3 us (4%)
    pallas_call x1, Pallas kernels, on_device(): pl.pallas_call(functools.partial(body, n, strength), out_shape=(out, out)...  25 us
    unnamed x11, local copies, waits for them, and re-layouts  3.64 us
    broadcast_in_dim x1, local copies, waits for them, and re-layouts, on_device(): cluster_order[None, :]  0.71 us

profile of v1, /device:TPU:0, one launch (start us, length us, event | category | flops | bytes accessed | tf_op | source)
XLA Modules:
  0.0 30.7 jit_solution(11898940928447180700)
XLA Ops:
  1.3 0.0 copy-start.3
  1.3 0.7 %broadcast_in_dim.7.order_ref = s32[1,1536]{1,0:T(1,128)S(1)} reshape(s32[1536]{0:T(1024)} %param.8) | data formatting | bytes 12288 | tf_op jit(solution)/shard_map/broadcast_in_dim | solution.py:324
  2.0 0.0 copy-done.3
  2.0 0.0 copy-start.2
  2.0 0.1 copy.8.cols_ref
  2.1 0.6 %copy-done.2 = f32[40]{0:T(128)S(1)} copy-done((f32[40]{0:T(128)S(1)}, f32[40]{0:T(128)}, u32[]{:S(2)}) %copy-start.2) | copy-done | bytes 184
  2.7 0.0 copy-start
  2.7 0.9 %copy-done = f32[40,1536]{1,0:T(8,128)S(1)} copy-done((f32[40,1536]{1,0:T(8,128)S(1)}, f32[40,1536]{1,0:T(8,128)}, u32[]{:S(2)}) %copy-start) | copy-done | bytes 245784
  3.6 0.0 copy-start.1
  3.6 0.8 %copy-done.1 = f32[8,1536]{1,0:T(8,128)S(1)} copy-done((f32[8,1536]{1,0:T(8,128)S(1)}, f32[8,1536]{1,0:T(8,128)}, u32[]{:S(2)}) %copy-start.1) | copy-done | bytes 49176
  4.4 25.0 %shard_map.77 = (f32[8,1536]{1,0:T(8,128)S(1)}, f32[8,1536]{1,0:T(8,128)S(1)}) custom-call(f32[40,1536]{1,0:T(8,128)S(1)} %copy-done, f32[1,40]{1,0:T(1,128)S(1)} %bitcast.1, s32[1,1536]{1,0:T(1,128)S(1)} %broadcast_in_dim.7.order_ref, s32[1]{0:T(128)S(6)} %copy.11.counts_ref, s32[12,3]{1,0:T(8,128)S(1)} %copy.8.cols_ref, f32[8,1536]{1,0:T(8,128)S(1)} %copy-done.1), custom_call_target="tpu_custom_call" | custom-call | tf_op jit(solution)/shard_map/pallas_call | solution.py:299
  29.4 0.6 %copy.12 = f32[8,1536]{1,0:T(8,128)} copy(f32[8,1536]{1,0:T(8,128)S(1)} %get-tuple-element.4) | data formatting | bytes 98304
  30.1 0.6 %copy.13 = f32[8,1536]{1,0:T(8,128)} copy(f32[8,1536]{1,0:T(8,128)S(1)} %get-tuple-element.5) | data formatting | bytes 98304
Async XLA Ops:
  1.3 0.7 %copy-start.3 = (s32[12,3]{0,1:T(4,128)S(1)}, s32[12,3]{0,1:T(4,128)}, u32[]{:S(2)}) copy-start(s32[12,3]{0,1:T(4,128)} %param.10) | copy-start | bytes 436
  2.0 0.7 %copy-start.2 = (f32[40]{0:T(128)S(1)}, f32[40]{0:T(128)}, u32[]{:S(2)}) copy-start(f32[40]{0:T(128)} %param.7) | copy-start | bytes 484
  2.7 0.9 %copy-start = (f32[40,1536]{1,0:T(8,128)S(1)}, f32[40,1536]{1,0:T(8,128)}, u32[]{:S(2)}) copy-start(f32[40,1536]{1,0:T(8,128)} %raw_ref.1) | copy-start | bytes 737284
  3.6 0.8 %copy-start.1 = (f32[8,1536]{1,0:T(8,128)S(1)}, f32[8,1536]{1,0:T(8,128)}, u32[]{:S(2)}) copy-start(f32[8,1536]{1,0:T(8,128)} %targ_ref.1) | copy-start | bytes 147460

commit v2 on v1

--- a/solution.py
+++ b/solution.py
@@ -14,6 +14,7 @@
 CHUNK = 64
 LANES = 128
 FEAT = 40
+VMEM_ASK = 65_200_000
 DEPTH = 256
 
 root_three = math.sqrt(3.0)
@@ -62,11 +63,18 @@
 
 
 def body(
-    n, strength, raw_ref, scale_ref, order_ref, counts_ref, cols_ref, targ_ref, sol_ref, res_ref,
-    feat, up_feat, r_buf, up_r, w_buf, up_w, out1, in1, out2, in2, part1, got1, part2, got2,
+    n, strength, raw_hbm, scale_ref, order_ref, counts_ref, cols_ref, targ_hbm, sol_ref, res_ref,
+    raw_ref, targ_ref, load_sem, feat, up_feat, r_buf, up_r, w_buf, up_w, out1, in1, out2, in2, part1, got1, part2, got2,
     a_ref, b_ref, ds_ref, khi, klo, vec, send_sem, recv_sem, psend1, precv1, psend2, precv2,
 ):
+    load_raw = pltpu.make_async_copy(raw_hbm, raw_ref, load_sem.at[0])
+    load_targ = pltpu.make_async_copy(targ_hbm, targ_ref, load_sem.at[1])
+    load_raw.start()
+    load_targ.start()
     me = lax.axis_index("pairs")
+    lane_rhs = lax.axis_index("rhs")
+    mine = lax.rem(lane_rhs, 2)
+    sibling = lane_rhs + 1 - 2 * mine
     mesh_ids = pl.DeviceIdType.MESH
     p_slots = NT * TILE
     has_up = me < n - 1
@@ -76,10 +84,10 @@
     for k in range(1, n):
         pl.semaphore_signal(barrier, inc=1, device_id={"pairs": lax.rem(me + k, n)}, device_id_type=mesh_ids)
 
+    pl.semaphore_signal(barrier, inc=1, device_id={"rhs": sibling}, device_id_type=mesh_ids)
+
     lane = lax.broadcasted_iota(jnp.int32, (8, p_slots), 1)
     live = jnp.where(lane < counts_ref[0], 1.0, 0.0)
-    r0 = targ_ref[...] * live
-    r_buf[...] = r0
 
     @pl.when(jnp.logical_not(has_up))
     def _():
@@ -98,7 +106,7 @@
     def gather_tile(i):
         for c in range(TILE // LANES):
             first = i * TILE + c * LANES
-            index = order_ref[:, first : first + LANES] - me * p_slots
+            index = order_ref[first // LANES : first // LANES + 1, :] - me * p_slots
             index = jnp.broadcast_to(index, (FEAT, LANES))
             group = lax.shift_right_logical(index, 7)
             within = jnp.bitwise_and(index, LANES - 1)
@@ -106,10 +114,11 @@
             for s in range(p_slots // LANES):
                 part = jnp.take_along_axis(raw_ref[:, s * LANES : (s + 1) * LANES], within, axis=1)
                 got = jnp.where(group == s, part, got)
-            feat[i, :, c * LANES : (c + 1) * LANES] = got * scale
-
+            feat[i, c // 2, :, c % 2 * LANES : (c % 2 + 1) * LANES] = got * scale
+
+    load_raw.wait()
     gather_tile(0)
-    pl.semaphore_wait(barrier, n - 1)
+    pl.semaphore_wait(barrier, n)
 
     def shift(src, dst, slot, by):
         return pltpu.make_async_remote_copy(
@@ -117,7 +126,22 @@
             device_id={"pairs": lax.rem(me + by + n, n)}, device_id_type=mesh_ids,
         )
 
-    c_feat = [shift(feat.at[i], up_feat.at[i], 4 + i, -1) for i in range(NT)]
+    c_feat = [shift(feat.at[i, mine], up_feat.at[i, mine], 4 + i, -1) for i in range(NT)]
+    c_hand = [
+        pltpu.make_async_remote_copy(
+            src_ref=up_feat.at[i, mine], dst_ref=up_feat.at[i, mine],
+            send_sem=send_sem.at[7 + i], recv_sem=recv_sem.at[7 + i],
+            device_id={"rhs": sibling}, device_id_type=mesh_ids,
+        )
+        for i in range(NT)
+    ]
+
+    def hand_on(i):
+        @pl.when(has_up)
+        def _():
+            c_feat[i].wait_recv()
+            c_hand[i].start()
+
     c_r = shift(r_buf, up_r, 0, -1)
     c_w = shift(w_buf, up_w, 1, -1)
     c_1 = shift(out1, in1, 2, 1)
@@ -139,6 +163,9 @@
     gather_tile(1)
     when_start(has_down, c_feat[1])
     gather_tile(2)
+    load_targ.wait()
+    r0 = targ_ref[...] * live
+    r_buf[...] = r0
     when_start(has_down, c_feat[2], c_r)
 
     base = me * NT
@@ -166,7 +193,7 @@
 
     for i in range(NT):
         span = slice(i * TILE, (i + 1) * TILE)
-        x = feat[i]
+        x = jnp.concatenate([feat[i, 0], feat[i, 1]], axis=1)
         a_ref[span, :] = operand(x, True).T.astype(bf16)
         b_ref[:, span] = operand(x, False).astype(bf16)
 
@@ -198,12 +225,17 @@
 
     for i in range(NT):
         form(i, i, b_ref[:, i * TILE : (i + 1) * TILE])
+    hand_on(0)
     form(NT, 0, pick(b_ref, 0, True))
+    hand_on(1)
     for i, pairs in ((0, (1, 2)), (1, (3, 4)), (2, (5,))):
-        when_recv(has_up, c_feat[i])
-        b_ref[:, p_slots + i * TILE : p_slots + (i + 1) * TILE] = operand(up_feat[i], False).astype(bf16)
+        when_recv(has_up, c_hand[i])
+        up_x = jnp.concatenate([up_feat[i, 0], up_feat[i, 1]], axis=1)
+        b_ref[:, p_slots + i * TILE : p_slots + (i + 1) * TILE] = operand(up_x, False).astype(bf16)
         for k in pairs:
             form(NT + k, OFF[k][0], pick(b_ref, k, False))
+        if i == 0:
+            hand_on(2)
 
     def own(i):
         return vec[:, i * TILE : (i + 1) * TILE]
@@ -276,7 +308,7 @@
 
     @pl.when(has_up)
     def _():
-        for c in (c_1, c_2):
+        for c in (c_1, c_2, *c_hand):
             c.wait_send()
 
     for c in sums1 + sums2:
@@ -291,6 +323,7 @@
     if rhs_rows < 8:
         padded = jnp.concatenate([targets, jnp.ones((8 - rhs_rows, p_slots), f32)], axis=0)
     vmem = pl.BlockSpec(memory_space=pltpu.VMEM)
+    hbm = pl.BlockSpec(memory_space=pltpu.HBM)
     smem = pl.BlockSpec(memory_space=pltpu.SMEM)
     field = pltpu.VMEM((8, p_slots), f32)
     dma = pltpu.SemaphoreType.DMA
@@ -299,11 +332,14 @@
     sol, res = pl.pallas_call(
         functools.partial(body, n, strength),
         out_shape=(out, out),
-        in_specs=[vmem, vmem, vmem, smem, smem, vmem],
+        in_specs=[hbm, vmem, vmem, smem, smem, hbm],
         out_specs=(vmem, vmem),
         scratch_shapes=[
-            pltpu.VMEM((NT, FEAT, TILE), f32),
-            pltpu.VMEM((NT, FEAT, TILE), f32),
+            pltpu.VMEM((FEAT, p_slots), f32),
+            field,
+            dma((2,)),
+            pltpu.VMEM((NT, 2, FEAT, TILE // 2), f32),
+            pltpu.VMEM((NT, 2, FEAT, TILE // 2), f32),
             field, field, field, field, field, field, field, field,
             pltpu.VMEM((16, 128), f32),
             pltpu.VMEM((n - 1, 16, 128), f32),
@@ -315,13 +351,13 @@
             pltpu.VMEM((tiles, TILE, TILE), bf16),
             pltpu.VMEM((tiles, TILE, TILE), bf16),
             pltpu.VMEM((16, 2 * p_slots), bf16),
-            dma((7,)), dma((7,)),
+            dma((10,)), dma((10,)),
             dma((n - 1,)), dma((n - 1,)), dma((n - 1,)), dma((n - 1,)),
         ],
         compiler_params=pltpu.CompilerParams(
-            collective_id=0, has_side_effects=True, vmem_limit_bytes=48 * 2**20
+            collective_id=0, has_side_effects=True, vmem_limit_bytes=VMEM_ASK
         ),
-    )(features, inv_scale[None, :], cluster_order[None, :], counts, tile_cols, padded)
+    )(features, inv_scale[None, :], cluster_order.reshape(p_slots // LANES, LANES), counts, tile_cols, padded)
     return sol[:rhs_rows], res[:rhs_rows]
 
 

time: 30.9 us -> 30.9 us (level)
  local copies, waits for them, and re-layouts: 4.35 us -> 3.42 us
  Pallas kernels: 25 us -> 25.9 us
    pallas_call x1, Pallas kernels: 25 us -> 25.9 us  [on_device(): pl.pallas_call(functools.partial(body, n, strength), out_shape=(out, out)...]
    broadcast_in_dim x1 -> x0, local copies, waits for them, and re-layouts: 0.71 us -> none  [on_device(): cluster_order[None, :]]
    unnamed x11 -> x7, local copies, waits for them, and re-layouts: 3.64 us -> 3.42 us
where the time goes in v2:
time: 30.9 us; the launch traced here: 30.6 us
  Pallas kernels  25.9 us (84%)
  local copies, waits for them, and re-layouts  3.42 us (11%)
  between operations  1.3 us (4%)
    pallas_call x1, Pallas kernels, on_device(): pl.pallas_call(functools.partial(body, n, strength), out_shape=(out, out)...  25.9 us
    unnamed x7, local copies, waits for them, and re-layouts  3.42 us

profile of v2, /device:TPU:0, one launch (start us, length us, event | category | flops | bytes accessed | tf_op | source)
XLA Modules:
  0.0 30.6 jit_solution(243488487608006138)
XLA Ops:
  1.3 0.0 copy-start.1
  1.3 0.7 %copy-done.1 = s32[12,3]{0,1:T(4,128)S(1)} copy-done((s32[12,3]{0,1:T(4,128)S(1)}, s32[12,3]{0,1:T(4,128)}, u32[]{:S(2)}) %copy-start.1) | copy-done | bytes 168
  2.0 0.7 %copy.8.cols_ref = s32[12,3]{1,0:T(8,128)} copy(s32[12,3]{0,1:T(4,128)S(1)} %copy-done.1) | data formatting | bytes 288 | tf_op args[4]
  2.6 25.9 %shard_map.77 = (f32[8,1536]{1,0:T(8,128)}, f32[8,1536]{1,0:T(8,128)}) custom-call(f32[40,1536]{1,0:T(8,128)} %raw_hbm.1, f32[1,40]{1,0:T(1,128)} %bitcast.3, s32[12,128]{1,0:T(8,128)} %bitcast.2, s32[1]{0:T(128)S(6)} %copy.11.counts_ref, s32[12,3]{1,0:T(8,128)} %copy.8.cols_ref, f32[8,1536]{1,0:T(8,128)} %targ_hbm.1), custom_call_target="tpu_custom_call" | custom-call | tf_op jit(solution)/shard_map/pallas_call | solution.py:332
  28.5 0.0 copy-start
  28.5 1.4 %copy.12 = f32[8,1536]{1,0:T(8,128)} copy(f32[8,1536]{1,0:T(8,128)} %get-tuple-element.4) | data formatting | bytes 98304
  30.0 0.0 copy-done
  30.0 0.6 %copy.13 = f32[8,1536]{1,0:T(8,128)} copy(f32[8,1536]{1,0:T(8,128)S(1)} %copy-done) | data formatting | bytes 98304
Async XLA Ops:
  1.3 0.7 %copy-start.1 = (s32[12,3]{0,1:T(4,128)S(1)}, s32[12,3]{0,1:T(4,128)}, u32[]{:S(2)}) copy-start(s32[12,3]{0,1:T(4,128)} %param.10) | copy-start | bytes 436
  28.5 1.4 %copy-start = (f32[8,1536]{1,0:T(8,128)S(1)}, f32[8,1536]{1,0:T(8,128)}, u32[]{:S(2)}) copy-start(f32[8,1536]{1,0:T(8,128)} %get-tuple-element.5) | copy-start | bytes 147460

commit v3 on v2

--- a/solution.py
+++ b/solution.py
@@ -14,7 +14,7 @@
 CHUNK = 64
 LANES = 128
 FEAT = 40
-VMEM_ASK = 65_200_000
+VMEM_ASK = 65_100_000
 DEPTH = 256
 
 root_three = math.sqrt(3.0)
@@ -65,7 +65,7 @@
 def body(
     n, strength, raw_hbm, scale_ref, order_ref, counts_ref, cols_ref, targ_hbm, sol_ref, res_ref,
     raw_ref, targ_ref, load_sem, feat, up_feat, r_buf, up_r, w_buf, up_w, out1, in1, out2, in2, part1, got1, part2, got2,
-    a_ref, b_ref, ds_ref, khi, klo, vec, send_sem, recv_sem, psend1, precv1, psend2, precv2,
+    a_ref, b_ref, ds_ref, khi, klo, vec, tall, send_sem, recv_sem, psend1, precv1, psend2, precv2,
 ):
     load_raw = pltpu.make_async_copy(raw_hbm, raw_ref, load_sem.at[0])
     load_targ = pltpu.make_async_copy(targ_hbm, targ_ref, load_sem.at[1])
@@ -171,8 +171,8 @@
     base = me * NT
     start, keep0, keep1 = [], [], []
     for row, cand, slot in OFF:
-        a = cols_ref[base + row, 1]
-        b = cols_ref[base + row, 2]
+        a = cols_ref[1, base + row]
+        b = cols_ref[2, base + row]
         a_in = jnp.where(a < 0, row + 3, a - base)
         b_in = jnp.where(b < 0, row + 3, b - base)
         if slot == 0:
@@ -209,13 +209,19 @@
             khi[t, at, :] = hi
             klo[t, at, :] = (k - hi.astype(f32)).astype(bf16)
 
-    nt_dims = (((1,), (1,)), ((), ()))
-
     def to_rows(t, v):
-        return fold(
-            lax.dot_general(v, khi[t], nt_dims, preferred_element_type=f32)
-            + lax.dot_general(v, klo[t], nt_dims, preferred_element_type=f32)
-        )
+        return jnp.dot(khi[t], v, preferred_element_type=f32) + jnp.dot(klo[t], v, preferred_element_type=f32)
+
+    def upright(v):
+        parts = two_parts(v).astype(f32)
+        wide = jnp.concatenate([parts, jnp.zeros((LANES - 16, p_slots), f32)], axis=0)
+        return wide.T.astype(bf16)
+
+    def pick_rows(k):
+        cand = OFF[k][1]
+        lo = tall[cand * TILE : (cand + 1) * TILE, :]
+        hi = tall[(cand + 1) * TILE : (cand + 2) * TILE, :]
+        return jnp.where(start[k] == cand, lo, hi)
 
     def to_cols(t, v):
         return fold(
@@ -242,6 +248,7 @@
 
     def operate(v, out_ref, c_out, up_ref, c_up, in_ref):
         vec[:, :p_slots] = two_parts(v)
+        tall[:p_slots, :] = upright(v)
         acc = [jnp.zeros((8, TILE), f32) for _ in range(2 * NT)]
         for k in range(1, 6):
             row, cand, _ = OFF[k]
@@ -251,16 +258,19 @@
         out_ref[...] = jnp.concatenate(acc[NT:], axis=1)
         when_start(has_up, c_out)
         for i in range(NT):
-            acc[i] = acc[i] + to_rows(i, own(i))
+            acc[i] = acc[i] + to_cols(i, own(i))
         t = to_cols(NT, own(0))
         acc[1] = acc[1] + keep0[0] * t
         acc[2] = acc[2] + keep1[0] * t
-        acc[0] = acc[0] + (keep0[0] + keep1[0]) * to_rows(NT, pick(vec, 0, True))
+        side = [(keep0[0] + keep1[0]) * to_rows(NT, pick_rows(0)), None, None]
         when_recv(has_up, c_up)
-        vec[:, p_slots:] = two_parts(up_ref[...])
+        tall[p_slots:, :] = upright(up_ref[...])
         for k in range(1, 6):
             row = OFF[k][0]
-            acc[row] = acc[row] + (keep0[k] + keep1[k]) * to_rows(NT + k, pick(vec, k, False))
+            t = (keep0[k] + keep1[k]) * to_rows(NT + k, pick_rows(k))
+            side[row] = t if side[row] is None else side[row] + t
+        for row in range(NT):
+            acc[row] = acc[row] + fold(side[row].T[:16])
         when_recv(has_down, c_out)
         total = jnp.concatenate(acc[:NT], axis=1) + in_ref[...]
         return v + strength * live * total
@@ -350,14 +360,15 @@
             pltpu.VMEM((2, TILE, TILE), f32),
             pltpu.VMEM((tiles, TILE, TILE), bf16),
             pltpu.VMEM((tiles, TILE, TILE), bf16),
-            pltpu.VMEM((16, 2 * p_slots), bf16),
+            pltpu.VMEM((16, p_slots), bf16),
+            pltpu.VMEM((2 * p_slots, LANES), bf16),
             dma((10,)), dma((10,)),
             dma((n - 1,)), dma((n - 1,)), dma((n - 1,)), dma((n - 1,)),
         ],
         compiler_params=pltpu.CompilerParams(
             collective_id=0, has_side_effects=True, vmem_limit_bytes=VMEM_ASK
         ),
-    )(features, inv_scale[None, :], cluster_order.reshape(p_slots // LANES, LANES), counts, tile_cols, padded)
+    )(features, inv_scale[None, :], cluster_order.reshape(p_slots // LANES, LANES), counts, tile_cols.T, padded)
     return sol[:rhs_rows], res[:rhs_rows]
 
 

time: 30.9 us -> 29.8 us (0.964)
  local copies, waits for them, and re-layouts: 3.42 us -> 2.06 us
    unnamed x7 -> x4, local copies, waits for them, and re-layouts: 3.42 us -> 2.06 us
    pallas_call x1, Pallas kernels: 25.9 us -> 26.2 us  [on_device(): pl.pallas_call(functools.partial(body, n, strength), out_shape=(out, out)...]
where the time goes in v3:
time: 29.8 us; the launch traced here: 29.6 us
  Pallas kernels  26.2 us (88%)
  local copies, waits for them, and re-layouts  2.06 us (7%)
  between operations  1.29 us (4%)
    pallas_call x1, Pallas kernels, on_device(): pl.pallas_call(functools.partial(body, n, strength), out_shape=(out, out)...  26.2 us
    unnamed x4, local copies, waits for them, and re-layouts  2.06 us

profile of v3, /device:TPU:0, one launch (start us, length us, event | category | flops | bytes accessed | tf_op | source)
XLA Modules:
  0.0 29.6 jit_solution(15992344601727628518)
XLA Ops:
  1.3 26.2 %shard_map.77 = (f32[8,1536]{1,0:T(8,128)}, f32[8,1536]{1,0:T(8,128)}) custom-call(f32[40,1536]{1,0:T(8,128)} %raw_hbm.1, f32[1,40]{1,0:T(1,128)} %bitcast.5, s32[12,128]{1,0:T(8,128)} %bitcast.3, s32[1]{0:T(128)S(6)} %copy.10.counts_ref, s32[3,12]{1,0:T(4,128)} %bitcast.4, f32[8,1536]{1,0:T(8,128)} %targ_hbm.1), custom_call_target="tpu_custom_call" | custom-call | tf_op jit(solution)/shard_map/pallas_call | solution.py:342
  27.5 0.0 copy-start
  27.5 1.4 %copy.11 = f32[8,1536]{1,0:T(8,128)} copy(f32[8,1536]{1,0:T(8,128)} %get-tuple-element.4) | data formatting | bytes 98304
  28.9 0.0 copy-done
  28.9 0.6 %copy.12 = f32[8,1536]{1,0:T(8,128)} copy(f32[8,1536]{1,0:T(8,128)S(1)} %copy-done) | data formatting | bytes 98304
Async XLA Ops:
  27.5 1.4 %copy-start = (f32[8,1536]{1,0:T(8,128)S(1)}, f32[8,1536]{1,0:T(8,128)}, u32[]{:S(2)}) copy-start(f32[8,1536]{1,0:T(8,128)} %get-tuple-element.5) | copy-start | bytes 147460

commit v4 on v3

--- a/solution.py
+++ b/solution.py
@@ -14,7 +14,7 @@
 CHUNK = 64
 LANES = 128
 FEAT = 40
-VMEM_ASK = 65_100_000
+VMEM_ASK = 64_980_000
 DEPTH = 256
 
 root_three = math.sqrt(3.0)

time: 29.8 us -> 29.8 us (level)
  no operation moved by 1% of the time
where the time goes in v4:
time: 29.8 us; the launch traced here: 29.6 us
  Pallas kernels  26.2 us (88%)
  local copies, waits for them, and re-layouts  2.06 us (7%)
  between operations  1.29 us (4%)
    pallas_call x1, Pallas kernels, on_device(): pl.pallas_call(functools.partial(body, n, strength), out_shape=(out, out)...  26.2 us
    unnamed x4, local copies, waits for them, and re-layouts  2.06 us

profile of v4, /device:TPU:0, one launch (start us, length us, event | category | flops | bytes accessed | tf_op | source)
XLA Modules:
  0.0 29.6 jit_solution(15992344601727628518)
XLA Ops:
  1.3 26.2 %shard_map.77 = (f32[8,1536]{1,0:T(8,128)}, f32[8,1536]{1,0:T(8,128)}) custom-call(f32[40,1536]{1,0:T(8,128)} %raw_hbm.1, f32[1,40]{1,0:T(1,128)} %bitcast.5, s32[12,128]{1,0:T(8,128)} %bitcast.3, s32[1]{0:T(128)S(6)} %copy.10.counts_ref, s32[3,12]{1,0:T(4,128)} %bitcast.4, f32[8,1536]{1,0:T(8,128)} %targ_hbm.1), custom_call_target="tpu_custom_call" | custom-call | tf_op jit(solution)/shard_map/pallas_call | solution.py:342
  27.5 0.0 copy-start
  27.5 1.4 %copy.11 = f32[8,1536]{1,0:T(8,128)} copy(f32[8,1536]{1,0:T(8,128)} %get-tuple-element.4) | data formatting | bytes 98304
  28.9 0.0 copy-done
  28.9 0.6 %copy.12 = f32[8,1536]{1,0:T(8,128)} copy(f32[8,1536]{1,0:T(8,128)S(1)} %copy-done) | data formatting | bytes 98304
Async XLA Ops:
  27.5 1.4 %copy-start = (f32[8,1536]{1,0:T(8,128)S(1)}, f32[8,1536]{1,0:T(8,128)}, u32[]{:S(2)}) copy-start(f32[8,1536]{1,0:T(8,128)} %get-tuple-element.5) | copy-start | bytes 147460
